TPU v7x, 128 devices: a whole 4x4x4 slice. The times are simulated.
128 devices in a mesh: gx: 32 (over z, y_lo, x), gy: 4 (over y_hi, core).
Axes of the slice: x: 4, y: 4 (y_hi: 2, y_lo: 2; y = y_hi * 2 + y_lo), z: 4, core: 2. Of those that a mesh axis runs over, the one named last changes fastest.
Arguments:
- fluid_source: float32 [256, 128, 512], P('gx', 'gy'), may hold values from -6 to 6
- fluid_diag: float32 [256, 128, 512], P('gx', 'gy'), may hold values from 0.05 to 2
- stiff_ref: float32 [81, 81], replicated
- elem_coef: float32 [49152], P(('gx', 'gy')), may hold values from 0.3 to 3
- connect: int32 [27, 49152], P(None, ('gx', 'gy')), may hold values from 0 to 12543
- live_count: int32 [128], P(('gx', 'gy')), may hold values from 48 to 384, as said below
- node_mass: float32 [393216], P(('gx', 'gy')), may hold values from 0.5 to 2
- solid_load: float32 [3, 393216], P(None, ('gx', 'gy')), may hold values from -24 to 24
- wet_normal: float32 [3, 32768], P(None, ('gx', 'gy')), may hold values from -6 to 6
- trac_face: int32 [4, 32768], P(None, ('gx', 'gy')), may hold values from 0 to 1023
- trac_weight: float32 [4, 32768], P(None, ('gx', 'gy')), may hold values from 0 to 0.5
- wall_node: int32 [4, 256, 128], P(None, 'gx', 'gy'), may hold values from 0 to 1023
- wall_weight: float32 [4, 256, 128], P(None, 'gx', 'gy'), may hold values from 0 to 0.5
Outputs:
- pressure: float32 [256, 128, 512], P('gx', 'gy')
- displacement: float32 [3, 393216], P(None, ('gx', 'gy'))
Inputs may be any that keep to these rules, and one draw needn't show every extreme that they name: `connect`: entries number columns of the extended node list of the element's segment: its 12288 own nodes, then the first 256 nodes of the next segment. `live_count`: live slots of each device come first in its 384 slots; some device is full. `trac_face`: indices into the wall faces of the node's span slab, in the order of wall_seg. `wall_node`: indices into the face's segment's list of 1024 wetted nodes.
All inputs are finite; a program needn't handle non-finite values.
Results may differ from a plain program's by a relative error of at most 0.00014.
Values sent between devices are 32-bit elements; how exact they have to be, the bound alone decides.
No kernel may reach another device: no remote copies, remote signals or barrier semaphores. Data moves between devices by JAX's collectives and lax.ppermute only.
A program may use at most 64 MiB of HBM per device.

v0:
```python
import jax
import jax.numpy as jnp
from jax import lax
from jax.sharding import PartitionSpec as P

PLANE = 256
BLK = 384
ITERS = 2
PSEUDO = 2
COUPLE = 2
pseudo_weight = 0.8
traction_scale = 30.0
motion_scale = 2.0
relax_weight = 0.5


def padded_2(block, sides, width):
    for axis, dim in sides:
        count = lax.axis_size(axis)
        forward = [(i, i + 1) for i in range(count - 1)]
        backward = [(target, source) for source, target in forward]
        low = lax.ppermute(
            lax.slice_in_dim(block, block.shape[dim] - width, None, axis=dim), axis, forward
        )
        high = lax.ppermute(lax.slice_in_dim(block, 0, width, axis=dim), axis, backward)
        block = jnp.concatenate([low, block, high], axis=dim)
    return block


def from_behind(value, axis, by):
    length = lax.axis_size(axis)
    pairs = [(i, i + by) for i in range(length) if 0 <= i + by < length]
    return lax.ppermute(value, axis, pairs)


def fluid_step(pressure, fluid_diag, forcing):
    framed = padded_2(pressure, (("gx", 0), ("gy", 1)), 1)
    padded = jnp.pad(framed, ((0, 0), (0, 0), (1, 1)))
    beside = padded[2:, 1:-1, 1:-1] + padded[:-2, 1:-1, 1:-1]
    beside = beside + padded[1:-1, 2:, 1:-1] + padded[1:-1, :-2, 1:-1]
    beside = beside + padded[1:-1, 1:-1, 2:] + padded[1:-1, 1:-1, :-2]
    center = 6.0 + fluid_diag
    applied = center * pressure - beside
    return pressure + pseudo_weight * (forcing - applied) / center


def global_sums(values):
    totals = lax.psum((values[0],), ("gx", "gy"))
    return totals


def conjugate(apply_fn, solid_force):
    solution = jnp.zeros_like(solid_force)
    residual = solid_force
    direction = residual
    norm_now = global_sums((jnp.sum(residual * residual),))[0]
    for iteration in range(ITERS):
        applied = apply_fn(direction)
        curvature = global_sums((jnp.sum(direction * applied),))[0]
        step_size = norm_now / curvature
        solution = solution + step_size * direction
        residual = residual - step_size * applied
        norm_next = global_sums((jnp.sum(residual * residual),))[0]
        direction = residual + norm_next / norm_now * direction
        norm_now = norm_next
    return solution


def local(
    fluid_source,
    fluid_diag,
    stiff_ref,
    elem_coef,
    connect,
    live_count,
    node_mass,
    solid_load,
    wet_normal,
    trac_face,
    trac_weight,
    wall_node,
    wall_weight,
):
    owned_nodes = node_mass.shape[0]
    wet_count = wet_normal.shape[1]
    elem_count = connect.shape[1]
    node_order = connect.shape[0]
    chord_parts = lax.axis_size("gy")
    seg_nodes = owned_nodes * chord_parts
    turn_width = BLK
    live_here = live_count[0]
    position = jnp.arange(elem_count, dtype=jnp.int32)
    elem_weight = elem_coef * (position < live_here).astype(jnp.float32)
    turn_count = elem_count // turn_width

    def element_terms(extended):

        def one_turn(turn_index, summed):
            gathered = extended[:, connect].reshape(3 * node_order, turn_width)
            product = jnp.dot(
                stiff_ref,
                gathered,
                precision=lax.Precision.HIGHEST,
                preferred_element_type=jnp.float32,
            )
            product = product * elem_weight[None, :]
            return summed.at[:, connect].add(product.reshape(3, node_order, turn_width))

        return lax.fori_loop(0, turn_count, one_turn, jnp.zeros(extended.shape, jnp.float32))

    def plane_terms(segment_vec):
        following = from_behind(segment_vec[:, :PLANE], "gx", -1)
        summed = element_terms(jnp.concatenate([segment_vec, following], axis=1))
        tail_part = from_behind(summed[:, seg_nodes:], "gx", 1)
        return summed[:, :seg_nodes].at[:, :PLANE].add(tail_part)

    def apply_fn(vector_in):
        segment_vec = lax.all_gather(vector_in, "gy", axis=1, tiled=True)
        return (
            lax.psum_scatter(plane_terms(segment_vec), "gy", scatter_dimension=1, tiled=True)
            + node_mass[None, :] * vector_in
        )

    displacement = jnp.zeros(solid_load.shape, jnp.float32)
    pressure = jnp.zeros(fluid_source.shape, jnp.float32)
    for coupling in range(COUPLE):
        motion = jnp.sum(wet_normal * displacement[:, :wet_count], axis=0)
        motion_all = lax.all_gather(motion, "gy", axis=0, tiled=True)
        wall_source = motion_scale * jnp.sum(wall_weight * motion_all[wall_node], axis=0)
        forcing = fluid_source.at[:, :, 0].add(wall_source)
        for pseudo_step in range(PSEUDO):
            pressure = fluid_step(pressure, fluid_diag, forcing)
        wall_all = lax.all_gather(pressure[:, :, 0].reshape(-1), "gy", axis=0, tiled=True)
        traction = jnp.sum(trac_weight * wall_all[trac_face], axis=0)
        solid_force = solid_load.at[:, :wet_count].add(
            traction_scale * traction[None, :] * wet_normal
        )
        solution = conjugate(apply_fn, solid_force)
        displacement = displacement + relax_weight * (solution - displacement)
    return (pressure, displacement)


def solution(mesh):
    in_specs = (
        P("gx", "gy", None),
        P("gx", "gy", None),
        P(),
        P(("gx", "gy")),
        P(None, ("gx", "gy")),
        P(("gx", "gy")),
        P(("gx", "gy")),
        P(None, ("gx", "gy")),
        P(None, ("gx", "gy")),
        P(None, ("gx", "gy")),
        P(None, ("gx", "gy")),
        P(None, "gx", "gy"),
        P(None, "gx", "gy"),
    )
    out_specs = (P("gx", "gy", None), P(None, ("gx", "gy")))
    return jax.shard_map(local, mesh=mesh, in_specs=in_specs, out_specs=out_specs, check_vma=False)
```

profile of v0, /device:TPU:1, one launch (start us, length us, event | category | flops | bytes accessed | tf_op | source)
XLA Modules:
  0.0 1283.9 jit_solution(11407972666191639603)
XLA Ops:
  16.6 7.8 all-gather
  31.3 5.0 collective-permute-start.3
  46.7 6.8 collective-permute-start.7
  56.0 6.6 all-gather.1
  67.9 7.5 all_gather.26
  84.6 22.8 %gather_fusion.2 = f32[10368,3]{1,0:T(8,128)} fusion(f32[3,12544]{0,1:T(8,128)} %copy.164, s32[11264]{0:T(1024)S(1)} %pad_clamp_fusion), kind=kCustom, calls=%fused_computation.2 | custom fusion | bytes 290304 | tf_op jit(solution)/shard_map/while/body/eval_jaxpr/gather | solution.py:99
  115.6 61.1 %scatter_custom_fusion = f32[3,12544]{0,1:T(8,128)} fusion(s32[10368]{0:T(1024)S(1)} %reshape.330, f32[10368,3]{1,0:T(8,128)} %bitcast.64, f32[]{:T(128)} %constant.216.clone.1), kind=kCustom, calls=%fused_computation.18 | custom fusion | flops 31104 | bytes 151040 | tf_op jit(solution)/shard_map/while/body/eval_jaxpr/scatter-add | solution.py:107
  181.9 4.7 slice.442
  188.9 77.8 %reduce-scatter.13.cloned.1.call-done = f32[3072,3]{1,0:T(8,128)} async-done(((f32[12288,3]{1,0:T(8,128)}), f32[3072,3]{1,0:T(8,128)}) %reduce-scatter.13.cloned.1.call-update) | async-done | bytes 36880
  269.4 65.1 %all-reduce.7 = (f32[]{:T(128)}, f32[]{:T(128)}) all-reduce(f32[]{:T(128)} %get-tuple-element.181, f32[]{:T(128)} %get-tuple-element.180), channel_id=1, replica_groups=mesh['gx'=32,'gy'=4] {'gx','gy'}, use_global_device_ids=true, to_apply=%region_5.6 | all-reduce | flops 2 | bytes 16 | tf_op jit(solution)/shard_map/psum | solution.py:48
  336.3 64.3 %psum.58 = f32[]{:T(128)} all-reduce(f32[]{:T(128)} %multiply_reduce_fusion.5), channel_id=1, replica_groups=mesh['gx'=32,'gy'=4] {'gx','gy'}, use_global_device_ids=true, to_apply=%region_12.13 | all-reduce | flops 1 | bytes 8 | tf_op jit(solution)/shard_map/psum | solution.py:48
  401.9 7.9 all_gather.27
  418.4 22.8 %gather_fusion.3 = f32[10368,3]{1,0:T(8,128)} fusion(f32[3,12544]{0,1:T(8,128)} %copy.168, s32[11264]{0:T(1024)S(1)} %pad_clamp_fusion), kind=kCustom, calls=%fused_computation.3 | custom fusion | bytes 290304 | tf_op jit(solution)/shard_map/while/body/eval_jaxpr/gather | solution.py:99
  449.4 61.1 %scatter_custom_fusion.1 = f32[3,12544]{0,1:T(8,128)} fusion(s32[10368]{0:T(1024)S(1)} %reshape.330, f32[10368,3]{1,0:T(8,128)} %bitcast.65, f32[]{:T(128)} %constant.216.clone.1), kind=kCustom, calls=%fused_computation.16 | custom fusion | flops 31104 | bytes 151040 | tf_op jit(solution)/shard_map/while/body/eval_jaxpr/scatter-add | solution.py:107
  513.1 4.7 slice.446
  534.3 52.5 %reduce-scatter.15.cloned.1.call-done = f32[3072,3]{1,0:T(8,128)} async-done(((f32[12288,3]{1,0:T(8,128)}), f32[3072,3]{1,0:T(8,128)}) %reduce-scatter.15.cloned.1.call-update) | async-done | bytes 36880
  589.9 65.1 %psum.59 = f32[]{:T(128)} all-reduce(f32[]{:T(128)} %multiply_reduce_fusion.4), channel_id=1, replica_groups=mesh['gx'=32,'gy'=4] {'gx','gy'}, use_global_device_ids=true, to_apply=%region_16.17 | all-reduce | flops 1 | bytes 8 | tf_op jit(solution)/shard_map/psum | solution.py:48
  656.4 7.0 all-gather.2
  684.5 7.0 all-gather.3
  696.8 7.6 all_gather.30
  713.4 22.8 %gather_fusion.6 = f32[10368,3]{1,0:T(8,128)} fusion(f32[3,12544]{0,1:T(8,128)} %copy.173, s32[11264]{0:T(1024)S(1)} %pad_clamp_fusion), kind=kCustom, calls=%fused_computation.6 | custom fusion | bytes 290304 | tf_op jit(solution)/shard_map/while/body/eval_jaxpr/gather | solution.py:99
  744.4 61.1 %scatter_custom_fusion.2 = f32[3,12544]{0,1:T(8,128)} fusion(s32[10368]{0:T(1024)S(1)} %reshape.330, f32[10368,3]{1,0:T(8,128)} %bitcast.66, f32[]{:T(128)} %constant.216.clone.1), kind=kCustom, calls=%fused_computation.14 | custom fusion | flops 31104 | bytes 151040 | tf_op jit(solution)/shard_map/while/body/eval_jaxpr/scatter-add | solution.py:107
  809.8 4.7 slice.460
  816.8 71.2 %reduce-scatter.17.cloned.1.call-done = f32[3072,3]{1,0:T(8,128)} async-done(((f32[12288,3]{1,0:T(8,128)}), f32[3072,3]{1,0:T(8,128)}) %reduce-scatter.17.cloned.1.call-update) | async-done | bytes 36880
  890.6 65.1 %all-reduce.6 = (f32[]{:T(128)}, f32[]{:T(128)}) all-reduce(f32[]{:T(128)} %get-tuple-element.179, f32[]{:T(128)} %get-tuple-element.178), channel_id=1, replica_groups=mesh['gx'=32,'gy'=4] {'gx','gy'}, use_global_device_ids=true, to_apply=%region_21.22 | all-reduce | flops 2 | bytes 16 | tf_op jit(solution)/shard_map/psum | solution.py:48
  957.5 63.8 %psum.62 = f32[]{:T(128)} all-reduce(f32[]{:T(128)} %multiply_reduce_fusion.1), channel_id=1, replica_groups=mesh['gx'=32,'gy'=4] {'gx','gy'}, use_global_device_ids=true, to_apply=%region_27.28 | all-reduce | flops 1 | bytes 8 | tf_op jit(solution)/shard_map/psum | solution.py:48
  1022.6 7.9 all_gather.31
  1039.1 22.8 %gather_fusion.7 = f32[10368,3]{1,0:T(8,128)} fusion(f32[3,12544]{0,1:T(8,128)} %copy.177, s32[11264]{0:T(1024)S(1)} %pad_clamp_fusion), kind=kCustom, calls=%fused_computation.7 | custom fusion | bytes 290304 | tf_op jit(solution)/shard_map/while/body/eval_jaxpr/gather | solution.py:99
  1070.1 61.1 %scatter_custom_fusion.3 = f32[3,12544]{0,1:T(8,128)} fusion(s32[10368]{0:T(1024)S(1)} %reshape.330, f32[10368,3]{1,0:T(8,128)} %bitcast.63, f32[]{:T(128)} %constant.216.clone.1), kind=kCustom, calls=%fused_computation.12 | custom fusion | flops 31104 | bytes 151040 | tf_op jit(solution)/shard_map/while/body/eval_jaxpr/scatter-add | solution.py:107
  1133.8 4.7 slice.464
  1140.8 66.8 %reduce-scatter.19.cloned.1.call-done = f32[3072,3]{1,0:T(8,128)} async-done(((f32[12288,3]{1,0:T(8,128)}), f32[3072,3]{1,0:T(8,128)}) %reduce-scatter.19.cloned.1.call-update) | async-done | bytes 36880
  1210.1 65.0 %psum.63 = f32[]{:T(128)} all-reduce(f32[]{:T(128)} %multiply_reduce_fusion), channel_id=1, replica_groups=mesh['gx'=32,'gy'=4] {'gx','gy'}, use_global_device_ids=true, to_apply=%region_31.0 | all-reduce | flops 1 | bytes 8 | tf_op jit(solution)/shard_map/psum | solution.py:48
  (191 shorter events, 178.7 us)
Async XLA Ops:
  7.2 104.4 %copy-start = (f32[81,81]{1,0:T(8,128)S(1)}, f32[81,81]{1,0:T(8,128)}, u32[]{:S(2)}) copy-start(f32[81,81]{1,0:T(8,128)} %param.31) | copy-start | bytes 78736
  7.2 259.6 %reduce-scatter.13.cloned.1.call-start = ((), (), s32[]{:S(2)}) async-start(), calls=%async_computation.4 | async-start | bytes 7864320
  9.1 20.0 %collective-permute-start = (f32[1,32,512]{2,1,0:T(8,128)S(1)}, f32[1,32,512]{2,1,0:T(8,128)S(1)}, u32[]{:S(2)}, u32[]{:S(2)}) collective-permute-start(f32[1,32,512]{2,1,0:T(8,128)S(1)} %broadcast.217), channel_id=1, source_target_pairs={{4,0},{8,4},{12,8},{16,12},{20,16},{24,20},{28,24},{32,28},{36,32}... | collective-permute-start | bytes 196616 | tf_op jit(solution)/shard_map/ppermute | solution.py:25
  10.4 18.7 %collective-permute-start.1 = (f32[1,32,512]{2,1,0:T(8,128)S(1)}, f32[1,32,512]{2,1,0:T(8,128)S(1)}, u32[]{:S(2)}, u32[]{:S(2)}) collective-permute-start(f32[1,32,512]{2,1,0:T(8,128)S(1)} %broadcast.217), channel_id=1, source_target_pairs={{0,4},{4,8},{8,12},{12,16},{16,20},{20,24},{24,28},{28,32},{32,36}... | collective-permute-start | bytes 196616 | tf_op jit(solution)/shard_map/ppermute | solution.py:22
  29.2 7.4 collective-permute-start.2
  31.3 5.9 collective-permute-start.3
  37.6 39.0 %copy-start.9 = (f32[384]{0:T(512)S(1)}, f32[384]{0:T(512)}, u32[]{:S(2)}) copy-start(f32[384]{0:T(512)} %param.32) | copy-start | bytes 4612
  38.1 5.3 collective-permute-start.4
  39.4 5.3 collective-permute-start.5
  44.8 10.1 collective-permute-start.6
  46.7 8.2 collective-permute-start.7
  75.3 5.0 collective-permute-start.8
  177.6 9.0 collective-permute-start.9
  186.7 82.0 %copy-start.3 = (f32[3072]{0:T(1024)S(1)}, f32[3072]{0:T(1024)}, u32[]{:S(2)}) copy-start(f32[3072]{0:T(1024)} %param.35) | copy-start | bytes 36868
  188.9 397.9 %reduce-scatter.15.cloned.1.call-start = ((), (), s32[]{:S(2)}) async-start(), calls=%async_computation.5 | async-start | bytes 7864320
  409.7 4.3 collective-permute-start.10
  511.4 6.4 collective-permute-start.11
  520.1 367.9 %reduce-scatter.17.cloned.1.call-start = ((), (), s32[]{:S(2)}) async-start(), calls=%async_computation.6 | async-start | bytes 7864320
  520.1 5.3 collective-permute-start.12
  521.4 5.3 collective-permute-start.13
  526.8 62.6 %collective-permute-start.14 = (f32[10,1,512]{2,1,0:T(1,128)S(1)}, f32[10,1,512]{2,1,0:T(1,128)S(1)}, u32[]{:S(2)}, u32[]{:S(2)}) collective-permute-start(f32[10,1,512]{2,1,0:T(1,128)S(1)} %get-tuple-element.189), channel_id=1, source_target_pairs={{1,0},{2,1},{3,2},{5,4},{6,5},{7,6},{9,8},{10,9},{11,10},{13,12},{... | collective-permute-start | bytes 61448 | tf_op jit(solution)/shard_map/ppermute | solution.py:25
  531.3 58.1 %collective-permute-start.15 = (f32[10,1,512]{2,1,0:T(1,128)S(1)}, f32[10,1,512]{2,1,0:T(1,128)S(1)}, u32[]{:S(2)}, u32[]{:S(2)}) collective-permute-start(f32[10,1,512]{2,1,0:T(1,128)S(1)} %get-tuple-element.188), channel_id=1, source_target_pairs={{0,1},{1,2},{2,3},{4,5},{5,6},{6,7},{8,9},{9,10},{10,11},{12,13},{... | collective-permute-start | bytes 61448 | tf_op jit(solution)/shard_map/ppermute | solution.py:22
  668.8 5.4 collective-permute-start.16
  670.1 5.3 collective-permute-start.17
  675.4 7.1 collective-permute-start.18
  678.6 4.7 collective-permute-start.19
  684.3 51.8 %copy-start.2 = (f32[8,32,512]{2,1,0:T(8,128)}, f32[8,32,512]{2,1,0:T(8,128)S(1)}, u32[]{:S(2)}) copy-start(f32[8,32,512]{2,1,0:T(8,128)S(1)} %fusion.26) | copy-start | bytes 1572868
  704.4 4.7 collective-permute-start.20
  806.4 8.1 collective-permute-start.21
  816.7 390.8 %reduce-scatter.19.cloned.1.call-start = ((), (), s32[]{:S(2)}) async-start(), calls=%async_computation.7 | async-start | bytes 7864320
  1030.4 4.3 collective-permute-start.22
  1132.1 6.4 collective-permute-start.23
  (6 other events, 96.1 us)
Sparse Core Ops, SparseCore 0:
  189.0 77.7 reduce-scatter.12
  520.2 66.5 reduce-scatter.14
  816.9 71.0 reduce-scatter.16
  1140.9 66.5 reduce-scatter.18
where the time goes:
time: 1290 us; the launch traced here: 1280 us
  blocking collectives  447 us (35%)
  waiting for transfers between devices  287 us (22%)
  other arithmetic  266 us (21%)
  local copies, waits for them, and re-layouts  191 us (15%)
  starting transfers between devices  68 us (5%)
  between operations  23.2 us (2%)
    psum x6, blocking collectives, global_sums(): totals = lax.psum((values[0],), ('gx', 'gy'))  388 us
    unnamed x8, waiting for transfers between devices  268 us
    scatter-add x4, other arithmetic, one_turn(): return summed.at[:, connect].add(product.reshape(3, node_order, turn_width))  245 us
    gather x8, local copies, waits for them, and re-layouts, one_turn(): gathered = extended[:, connect].reshape(3 * node_order, turn_width)  108 us
    ppermute x8, starting transfers between devices, padded_2(): lax.ppermute(lax.slice_in_dim(block, block.shape[dim] - width, None, axis...  35.2 us
    all_gather x4, blocking collectives, apply_fn(): segment_vec = lax.all_gather(vector_in, 'gy', axis=1, tiled=True)  30.8 us
  transfers between devices with their start and end apart: 28, of which 14 were waited for; matrix products, arithmetic and copies ran while one was open for 2% of the time, Pallas kernels for 0%

commit v1 on v0

--- a/solution.py
+++ b/solution.py
@@ -1,3 +1,4 @@
+import functools
 import jax
 import jax.numpy as jnp
 from jax import lax
@@ -12,6 +13,15 @@
 traction_scale = 30.0
 motion_scale = 2.0
 relax_weight = 0.5
+
+
+def seats_all_order(page, along_axis, across):
+    for to_i in (along_axis, across):
+        page = lax.psum(page, to_i)
+    return page
+
+
+_switch_levels_all = functools.partial(seats_all_order, along_axis="gx", across="gy")
 
 
 def padded_2(block, sides, width):
@@ -45,7 +55,7 @@
 
 
 def global_sums(values):
-    totals = lax.psum((values[0],), ("gx", "gy"))
+    totals = _switch_levels_all((values[0],))
     return totals
 
 

time: 1290 us -> 1410 us (1.093)
  blocking collectives: 447 us -> 590 us
  waiting for transfers between devices: 287 us -> 268 us
    psum x6 -> x12, blocking collectives: 388 us -> 532 us  [seats_all_order(): page = lax.psum(page, to_i)]
    unnamed x8, waiting for transfers between devices: 268 us -> 249 us
where the time goes in v1:
time: 1410 us
  blocking collectives  590 us (42%)
  waiting for transfers between devices  268 us (19%)
  other arithmetic  266 us (19%)
  local copies, waits for them, and re-layouts  191 us (14%)
  starting transfers between devices  72.2 us (5%)
  between operations  23 us (2%)
    psum x12, blocking collectives, seats_all_order(): page = lax.psum(page, to_i)  532 us
    unnamed x8, waiting for transfers between devices  249 us
    scatter-add x4, other arithmetic, one_turn(): return summed.at[:, connect].add(product.reshape(3, node_order, turn_width))  245 us
    gather x8, local copies, waits for them, and re-layouts, one_turn(): gathered = extended[:, connect].reshape(3 * node_order, turn_width)  108 us
    ppermute x8, starting transfers between devices, padded_2(): lax.ppermute(lax.slice_in_dim(block, block.shape[dim] - width, None, axis...  35.7 us
    all_gather x4, blocking collectives, apply_fn(): segment_vec = lax.all_gather(vector_in, 'gy', axis=1, tiled=True)  30.1 us
  transfers between devices with their start and end apart: 28, of which 14 were waited for; matrix products, arithmetic and copies ran while one was open for 2% of the time, Pallas kernels for 0%

profile of v1, /device:TPU:1, one launch (start us, length us, event | category | flops | bytes accessed | tf_op | source)
XLA Modules:
  0.0 1412.1 jit_solution(16626982001988713694)
XLA Ops:
  16.6 7.8 all-gather
  46.7 6.8 collective-permute-start.7
  67.9 7.5 all_gather.26
  84.6 22.8 %gather_fusion.2 = f32[10368,3]{1,0:T(8,128)} fusion(f32[3,12544]{0,1:T(8,128)} %copy.164, s32[11264]{0:T(1024)S(1)} %pad_clamp_fusion), kind=kCustom, calls=%fused_computation.2 | custom fusion | bytes 290304 | tf_op jit(solution)/shard_map/while/body/eval_jaxpr/gather | solution.py:109
  115.6 61.1 %scatter_custom_fusion = f32[3,12544]{0,1:T(8,128)} fusion(s32[10368]{0:T(1024)S(1)} %reshape.330, f32[10368,3]{1,0:T(8,128)} %bitcast.64, f32[]{:T(128)} %constant.216.clone.1), kind=kCustom, calls=%fused_computation.18 | custom fusion | flops 31104 | bytes 151040 | tf_op jit(solution)/shard_map/while/body/eval_jaxpr/scatter-add | solution.py:117
  188.9 77.8 %reduce-scatter.13.cloned.1.call-done = f32[3072,3]{1,0:T(8,128)} async-done(((f32[12288,3]{1,0:T(8,128)}), f32[3072,3]{1,0:T(8,128)}) %reduce-scatter.13.cloned.1.call-update) | async-done | bytes 36880
  269.3 68.4 %all-reduce.7 = (f32[]{:T(128)}, f32[]{:T(128)}) all-reduce(f32[]{:T(128)} %get-tuple-element.181, f32[]{:T(128)} %get-tuple-element.180), channel_id=1, replica_groups=mesh['gx'=32,'gy'=4] {'gx'}, use_global_device_ids=true, to_apply=%region_5.6 | all-reduce | flops 2 | bytes 16 | tf_op jit(solution)/shard_map/psum | solution.py:20
  337.7 22.0 %all-reduce.9 = (f32[]{:T(128)}, f32[]{:T(128)}) all-reduce(f32[]{:T(128)} %get-tuple-element.184, f32[]{:T(128)} %get-tuple-element.185), channel_id=1, replica_groups=mesh['gx'=32,'gy'=4] {'gy'}, use_global_device_ids=true, to_apply=%region_6.7 | all-reduce | flops 2 | bytes 16 | tf_op jit(solution)/shard_map/psum | solution.py:20
  361.6 63.5 %psum.116 = f32[]{:T(128)} all-reduce(f32[]{:T(128)} %multiply_reduce_fusion.5), channel_id=1, replica_groups=mesh['gx'=32,'gy'=4] {'gx'}, use_global_device_ids=true, to_apply=%region_14.15 | all-reduce | flops 1 | bytes 8 | tf_op jit(solution)/shard_map/psum | solution.py:20
  425.1 21.7 %psum.117 = f32[]{:T(128)} all-reduce(f32[]{:T(128)} %psum.116), channel_id=1, replica_groups=mesh['gx'=32,'gy'=4] {'gy'}, use_global_device_ids=true, to_apply=%region_15.16 | all-reduce | flops 1 | bytes 8 | tf_op jit(solution)/shard_map/psum | solution.py:20
  448.1 7.6 all_gather.27
  464.6 22.8 %gather_fusion.3 = f32[10368,3]{1,0:T(8,128)} fusion(f32[3,12544]{0,1:T(8,128)} %copy.168, s32[11264]{0:T(1024)S(1)} %pad_clamp_fusion), kind=kCustom, calls=%fused_computation.3 | custom fusion | bytes 290304 | tf_op jit(solution)/shard_map/while/body/eval_jaxpr/gather | solution.py:109
  495.6 61.1 %scatter_custom_fusion.1 = f32[3,12544]{0,1:T(8,128)} fusion(s32[10368]{0:T(1024)S(1)} %reshape.330, f32[10368,3]{1,0:T(8,128)} %bitcast.65, f32[]{:T(128)} %constant.216.clone.1), kind=kCustom, calls=%fused_computation.16 | custom fusion | flops 31104 | bytes 151040 | tf_op jit(solution)/shard_map/while/body/eval_jaxpr/scatter-add | solution.py:117
  582.9 46.7 %reduce-scatter.15.cloned.1.call-done = f32[3072,3]{1,0:T(8,128)} async-done(((f32[12288,3]{1,0:T(8,128)}), f32[3072,3]{1,0:T(8,128)}) %reduce-scatter.15.cloned.1.call-update) | async-done | bytes 36880
  632.2 68.3 %psum.118 = f32[]{:T(128)} all-reduce(f32[]{:T(128)} %multiply_reduce_fusion.4), channel_id=1, replica_groups=mesh['gx'=32,'gy'=4] {'gx'}, use_global_device_ids=true, to_apply=%region_19.20 | all-reduce | flops 1 | bytes 8 | tf_op jit(solution)/shard_map/psum | solution.py:20
  700.9 22.0 %psum.119 = f32[]{:T(128)} all-reduce(f32[]{:T(128)} %psum.118), channel_id=1, replica_groups=mesh['gx'=32,'gy'=4] {'gy'}, use_global_device_ids=true, to_apply=%region_20.0 | all-reduce | flops 1 | bytes 8 | tf_op jit(solution)/shard_map/psum | solution.py:20
  724.4 7.0 all-gather.2
  752.5 7.0 all-gather.3
  764.8 7.5 all_gather.30
  781.2 22.8 %gather_fusion.6 = f32[10368,3]{1,0:T(8,128)} fusion(f32[3,12544]{0,1:T(8,128)} %copy.173, s32[11264]{0:T(1024)S(1)} %pad_clamp_fusion), kind=kCustom, calls=%fused_computation.6 | custom fusion | bytes 290304 | tf_op jit(solution)/shard_map/while/body/eval_jaxpr/gather | solution.py:109
  812.2 61.1 %scatter_custom_fusion.2 = f32[3,12544]{0,1:T(8,128)} fusion(s32[10368]{0:T(1024)S(1)} %reshape.330, f32[10368,3]{1,0:T(8,128)} %bitcast.66, f32[]{:T(128)} %constant.216.clone.1), kind=kCustom, calls=%fused_computation.14 | custom fusion | flops 31104 | bytes 151040 | tf_op jit(solution)/shard_map/while/body/eval_jaxpr/scatter-add | solution.py:117
  884.6 63.1 %reduce-scatter.17.cloned.1.call-done = f32[3072,3]{1,0:T(8,128)} async-done(((f32[12288,3]{1,0:T(8,128)}), f32[3072,3]{1,0:T(8,128)}) %reduce-scatter.17.cloned.1.call-update) | async-done | bytes 36880
  950.3 68.4 %all-reduce.6 = (f32[]{:T(128)}, f32[]{:T(128)}) all-reduce(f32[]{:T(128)} %get-tuple-element.179, f32[]{:T(128)} %get-tuple-element.178), channel_id=1, replica_groups=mesh['gx'=32,'gy'=4] {'gx'}, use_global_device_ids=true, to_apply=%region_25.26 | all-reduce | flops 2 | bytes 16 | tf_op jit(solution)/shard_map/psum | solution.py:20
  1018.7 22.0 %all-reduce.8 = (f32[]{:T(128)}, f32[]{:T(128)}) all-reduce(f32[]{:T(128)} %get-tuple-element.182, f32[]{:T(128)} %get-tuple-element.183), channel_id=1, replica_groups=mesh['gx'=32,'gy'=4] {'gy'}, use_global_device_ids=true, to_apply=%region_26.27 | all-reduce | flops 2 | bytes 16 | tf_op jit(solution)/shard_map/psum | solution.py:20
  1042.6 63.5 %psum.124 = f32[]{:T(128)} all-reduce(f32[]{:T(128)} %multiply_reduce_fusion.1), channel_id=1, replica_groups=mesh['gx'=32,'gy'=4] {'gx'}, use_global_device_ids=true, to_apply=%region_33.34 | all-reduce | flops 1 | bytes 8 | tf_op jit(solution)/shard_map/psum | solution.py:20
  1106.1 21.7 %psum.125 = f32[]{:T(128)} all-reduce(f32[]{:T(128)} %psum.124), channel_id=1, replica_groups=mesh['gx'=32,'gy'=4] {'gy'}, use_global_device_ids=true, to_apply=%region_34.35 | all-reduce | flops 1 | bytes 8 | tf_op jit(solution)/shard_map/psum | solution.py:20
  1129.1 7.6 all_gather.31
  1145.6 22.8 %gather_fusion.7 = f32[10368,3]{1,0:T(8,128)} fusion(f32[3,12544]{0,1:T(8,128)} %copy.177, s32[11264]{0:T(1024)S(1)} %pad_clamp_fusion), kind=kCustom, calls=%fused_computation.7 | custom fusion | bytes 290304 | tf_op jit(solution)/shard_map/while/body/eval_jaxpr/gather | solution.py:109
  1176.6 61.1 %scatter_custom_fusion.3 = f32[3,12544]{0,1:T(8,128)} fusion(s32[10368]{0:T(1024)S(1)} %reshape.330, f32[10368,3]{1,0:T(8,128)} %bitcast.63, f32[]{:T(128)} %constant.216.clone.1), kind=kCustom, calls=%fused_computation.12 | custom fusion | flops 31104 | bytes 151040 | tf_op jit(solution)/shard_map/while/body/eval_jaxpr/scatter-add | solution.py:117
  1248.9 61.7 %reduce-scatter.19.cloned.1.call-done = f32[3072,3]{1,0:T(8,128)} async-done(((f32[12288,3]{1,0:T(8,128)}), f32[3072,3]{1,0:T(8,128)}) %reduce-scatter.19.cloned.1.call-update) | async-done | bytes 36880
  1313.2 68.3 %psum.126 = f32[]{:T(128)} all-reduce(f32[]{:T(128)} %multiply_reduce_fusion), channel_id=1, replica_groups=mesh['gx'=32,'gy'=4] {'gx'}, use_global_device_ids=true, to_apply=%region_38.39 | all-reduce | flops 1 | bytes 8 | tf_op jit(solution)/shard_map/psum | solution.py:20
  1381.5 22.1 %psum.127 = f32[]{:T(128)} all-reduce(f32[]{:T(128)} %psum.126), channel_id=1, replica_groups=mesh['gx'=32,'gy'=4] {'gy'}, use_global_device_ids=true, to_apply=%region_39.40 | all-reduce | flops 1 | bytes 8 | tf_op jit(solution)/shard_map/psum | solution.py:20
  (197 shorter events, 213.6 us)
Async XLA Ops:
  7.2 104.4 %copy-start = (f32[81,81]{1,0:T(8,128)S(1)}, f32[81,81]{1,0:T(8,128)}, u32[]{:S(2)}) copy-start(f32[81,81]{1,0:T(8,128)} %param.31) | copy-start | bytes 78736
  7.2 259.6 %reduce-scatter.13.cloned.1.call-start = ((), (), s32[]{:S(2)}) async-start(), calls=%async_computation.4 | async-start | bytes 7864320
  9.1 20.0 %collective-permute-start = (f32[1,32,512]{2,1,0:T(8,128)S(1)}, f32[1,32,512]{2,1,0:T(8,128)S(1)}, u32[]{:S(2)}, u32[]{:S(2)}) collective-permute-start(f32[1,32,512]{2,1,0:T(8,128)S(1)} %broadcast.217), channel_id=1, source_target_pairs={{4,0},{8,4},{12,8},{16,12},{20,16},{24,20},{28,24},{32,28},{36,32}... | collective-permute-start | bytes 196616 | tf_op jit(solution)/shard_map/ppermute | solution.py:35
  10.4 18.7 %collective-permute-start.1 = (f32[1,32,512]{2,1,0:T(8,128)S(1)}, f32[1,32,512]{2,1,0:T(8,128)S(1)}, u32[]{:S(2)}, u32[]{:S(2)}) collective-permute-start(f32[1,32,512]{2,1,0:T(8,128)S(1)} %broadcast.217), channel_id=1, source_target_pairs={{0,4},{4,8},{8,12},{12,16},{16,20},{20,24},{24,28},{28,32},{32,36}... | collective-permute-start | bytes 196616 | tf_op jit(solution)/shard_map/ppermute | solution.py:32
  29.2 7.4 collective-permute-start.2
  31.3 5.9 collective-permute-start.3
  37.6 39.0 %copy-start.9 = (f32[384]{0:T(512)S(1)}, f32[384]{0:T(512)}, u32[]{:S(2)}) copy-start(f32[384]{0:T(512)} %param.32) | copy-start | bytes 4612
  38.1 5.3 collective-permute-start.4
  39.4 5.3 collective-permute-start.5
  44.8 10.1 collective-permute-start.6
  46.7 8.2 collective-permute-start.7
  75.3 5.0 collective-permute-start.8
  177.6 9.0 collective-permute-start.9
  186.7 82.0 %copy-start.3 = (f32[3072]{0:T(1024)S(1)}, f32[3072]{0:T(1024)}, u32[]{:S(2)}) copy-start(f32[3072]{0:T(1024)} %param.35) | copy-start | bytes 36868
  188.9 440.7 %reduce-scatter.15.cloned.1.call-start = ((), (), s32[]{:S(2)}) async-start(), calls=%async_computation.5 | async-start | bytes 7864320
  455.7 4.6 collective-permute-start.10
  557.6 8.1 collective-permute-start.11
  568.0 379.8 %reduce-scatter.17.cloned.1.call-start = ((), (), s32[]{:S(2)}) async-start(), calls=%async_computation.6 | async-start | bytes 7864320
  568.0 5.3 collective-permute-start.12
  569.3 5.3 collective-permute-start.13
  574.7 125.8 %collective-permute-start.14 = (f32[10,1,512]{2,1,0:T(1,128)S(1)}, f32[10,1,512]{2,1,0:T(1,128)S(1)}, u32[]{:S(2)}, u32[]{:S(2)}) collective-permute-start(f32[10,1,512]{2,1,0:T(1,128)S(1)} %get-tuple-element.193), channel_id=1, source_target_pairs={{1,0},{2,1},{3,2},{5,4},{6,5},{7,6},{9,8},{10,9},{11,10},{13,12},{... | collective-permute-start | bytes 61448 | tf_op jit(solution)/shard_map/ppermute | solution.py:35
  579.3 121.2 %collective-permute-start.15 = (f32[10,1,512]{2,1,0:T(1,128)S(1)}, f32[10,1,512]{2,1,0:T(1,128)S(1)}, u32[]{:S(2)}, u32[]{:S(2)}) collective-permute-start(f32[10,1,512]{2,1,0:T(1,128)S(1)} %get-tuple-element.192), channel_id=1, source_target_pairs={{0,1},{1,2},{2,3},{4,5},{5,6},{6,7},{8,9},{9,10},{10,11},{12,13},{... | collective-permute-start | bytes 61448 | tf_op jit(solution)/shard_map/ppermute | solution.py:32
  736.8 5.4 collective-permute-start.16
  738.1 5.3 collective-permute-start.17
  743.4 7.1 collective-permute-start.18
  746.6 4.7 collective-permute-start.19
  752.3 51.7 %copy-start.2 = (f32[8,32,512]{2,1,0:T(8,128)}, f32[8,32,512]{2,1,0:T(8,128)S(1)}, u32[]{:S(2)}) copy-start(f32[8,32,512]{2,1,0:T(8,128)S(1)} %fusion.26) | copy-start | bytes 1572868
  772.2 4.7 collective-permute-start.20
  874.2 8.1 collective-permute-start.21
  884.6 426.0 %reduce-scatter.19.cloned.1.call-start = ((), (), s32[]{:S(2)}) async-start(), calls=%async_computation.7 | async-start | bytes 7864320
  1136.7 4.6 collective-permute-start.22
  1238.6 8.1 collective-permute-start.23
  (6 other events, 96.1 us)
Sparse Core Ops, SparseCore 0:
  189.0 77.7 reduce-scatter.12
  568.1 61.4 reduce-scatter.14
  884.7 63.0 reduce-scatter.16
  1249.1 61.4 reduce-scatter.18
